TPU v7x, 32 devices: a whole 2x2x4 slice. The times are simulated.
32 devices in a mesh: row: 4 (over z), col: 4 (over y, x), ch: 2 (over core).
Axes of the slice: x: 2, y: 2, z: 4, core: 2. Of those that a mesh axis runs over, the one named last changes fastest.
Arguments:
- field: float32 [32, 512, 2048], P(None, 'row', 'col'), may hold values from -6 to 6
- spec_weight: float32 [2, 32, 32, 512], replicated, may hold values from -0.75 to 0.75
- point_weight: float32 [32, 32], replicated, may hold values from -1 to 1
- bias: float32 [32], P('ch'), may hold values from -1 to 1
- kept_modes: int32 [32], replicated, may hold values from 8 to 16, as said below
- residual: float32 [32, 16384], P('ch', ('row', 'col')), may hold values from -6 to 6
- trace_dest: int32 [16384, 1], P(('row', 'col')), may hold values from 0 to 15; in each aligned block of 1024 rows (0 to 1023, 1024 to 2047, ...) at most 128 rows name the same one
- trace_cell: int32 [16384], P(('row', 'col')), may hold values from 0 to 65535
Outputs:
- grad_field: float32 [32, 512, 2048], P('ch', 'row', 'col')
- grad_spec: float32 [2, 32, 32, 512], P(None, None, 'ch')
- grad_point: float32 [32, 32], P(None, 'ch')
- grad_bias: float32 [32], P('ch')
Inputs may be any that keep to these rules, and one draw needn't show every extreme that they name: `trace_dest`: of the 1024 points of one device, at most 128 go to one tile. `kept_modes`: some channel keeps 16 and some keeps 16 // 2.
All inputs are finite; a program needn't handle non-finite values.
Results may differ from a plain program's by a relative error of at most 0.00012.
Values sent between devices are 32-bit elements; how exact they have to be, the bound alone decides.
A program may use at most 192 MiB of HBM per device.

v0:
```python
import math
import jax
import jax.numpy as jnp
from jax import lax
from jax.sharding import PartitionSpec as P

C = 32
M = 16
RD = 128
CD = 512
P_DEV = 1024
MODES = 512
full_turn = 6.283185307179586
exact_mode = lax.Precision.HIGHEST


def row_angles(start_at, extent, period):
    frequency = jnp.arange(2 * M, dtype=jnp.int32)
    frequency = jnp.where(frequency < M, frequency, frequency - 2 * M)
    places = start_at + jnp.arange(extent, dtype=jnp.int32)
    phases = frequency[:, None] * places[None, :] % period
    angles = phases.astype(jnp.float32) * (full_turn / period)
    return (jnp.cos(angles), jnp.sin(angles))


def col_angles(start_at, extent, period):
    frequency = jnp.arange(M, dtype=jnp.int32)
    places = start_at + jnp.arange(extent, dtype=jnp.int32)
    phases = places[:, None] * frequency[None, :] % period
    angles = phases.astype(jnp.float32) * (full_turn / period)
    return (jnp.cos(angles), jnp.sin(angles))


def mode_mask(kept_modes):
    indices = jnp.arange(MODES, dtype=jnp.int32)
    row_mode = indices // M
    col_mode = indices % M
    row_rank = jnp.where(row_mode < M, row_mode, 2 * M - 1 - row_mode)
    allowed = (row_rank[None, :] < kept_modes[:, None]) & (col_mode[None, :] < kept_modes[:, None])
    return allowed.astype(jnp.float32)


def widen(values, full_size, along):
    shape_full = list(values.shape)
    block_size = values.shape[along]
    shape_full[along] = full_size
    holder = jnp.zeros(tuple(shape_full), jnp.float32)
    return lax.dynamic_update_slice_in_dim(holder, values, lax.axis_index("ch") * block_size, along)


def local_modes(own_field, scale_by):
    channel_count, row_count, col_count = own_field.shape
    row_devices = lax.axis_size("row")
    height = row_count * row_devices
    breadth = col_count * lax.axis_size("col")
    row_place = lax.axis_index("row")
    cos_rows, sin_rows = row_angles(row_place * row_count, row_count, height)
    real_rows = jnp.einsum("ar,crs->cas", cos_rows, own_field, precision=exact_mode)
    imag_rows = -jnp.einsum("ar,crs->cas", sin_rows, own_field, precision=exact_mode)
    col_first = lax.axis_index("col") * col_count
    cos_cols, sin_cols = col_angles(col_first, col_count, breadth)
    mode_re = jnp.einsum("cas,sb->cab", real_rows, cos_cols, precision=exact_mode) + jnp.einsum(
        "cas,sb->cab", imag_rows, sin_cols, precision=exact_mode
    )
    mode_im = jnp.einsum("cas,sb->cab", imag_rows, cos_cols, precision=exact_mode) - jnp.einsum(
        "cas,sb->cab", real_rows, sin_cols, precision=exact_mode
    )
    return (
        mode_re.reshape(channel_count, MODES) * scale_by,
        mode_im.reshape(channel_count, MODES) * scale_by,
    )


def tile_field(mode_re, mode_im, scale_by):
    channel_count = mode_re.shape[0]
    grid_re = mode_re.reshape(channel_count, 2 * M, M)
    grid_im = mode_im.reshape(channel_count, 2 * M, M)
    height = RD * lax.axis_size("row")
    breadth = CD * lax.axis_size("col")
    cos_cols, sin_cols = col_angles(lax.axis_index("col") * CD, CD, breadth)
    half_re = jnp.einsum("cab,sb->cas", grid_re, cos_cols, precision=exact_mode) - jnp.einsum(
        "cab,sb->cas", grid_im, sin_cols, precision=exact_mode
    )
    half_im = jnp.einsum("cab,sb->cas", grid_re, sin_cols, precision=exact_mode) + jnp.einsum(
        "cab,sb->cas", grid_im, cos_cols, precision=exact_mode
    )
    cos_rows, sin_rows = row_angles(lax.axis_index("row") * RD, RD, height)
    result = jnp.einsum("ar,cas->crs", cos_rows, half_re, precision=exact_mode) - jnp.einsum(
        "ar,cas->crs", sin_rows, half_im, precision=exact_mode
    )
    return result * scale_by


def per_device(
    field, spec_weight, point_weight, bias, kept_modes, residual, trace_dest, trace_cell
):
    channel_count = C // lax.axis_size("ch")
    own_first = lax.axis_index("ch") * channel_count
    row_devices = lax.axis_size("row")
    col_devices = lax.axis_size("col")
    tiles_all = row_devices * col_devices
    points_all = P_DEV * tiles_all
    capacity = max(2, 2 * P_DEV // tiles_all)
    forward_scale = 1.0 / math.sqrt(RD * row_devices * CD * col_devices)
    mix_scale = 1.0 / math.sqrt(MODES)
    own_field = lax.dynamic_slice_in_dim(field, own_first, channel_count, 0)
    part_re, part_im = local_modes(own_field, forward_scale)
    spec_re, spec_im = lax.psum((widen(part_re, C, 0), widen(part_im, C, 0)), ("row", "col", "ch"))
    allowed = mode_mask(kept_modes)
    weight_re = spec_weight[0] * allowed[None, :, :]
    weight_im = spec_weight[1] * allowed[None, :, :]
    out_wre = lax.dynamic_slice_in_dim(weight_re, own_first, channel_count, 1)
    out_wim = lax.dynamic_slice_in_dim(weight_im, own_first, channel_count, 1)
    mixed_re = jnp.sum(out_wre * spec_re[:, None, :] - out_wim * spec_im[:, None, :], axis=0)
    mixed_im = jnp.sum(out_wre * spec_im[:, None, :] + out_wim * spec_re[:, None, :], axis=0)
    out_point = lax.dynamic_slice_in_dim(point_weight, own_first, channel_count, 1)
    pre_act = (
        tile_field(mixed_re, mixed_im, mix_scale)
        + jnp.einsum("co,crs->ors", out_point, field, precision=exact_mode)
        + bias[:, None, None]
    )
    targets = trace_dest[:, 0]
    one_hot = (targets[:, None] == jnp.arange(tiles_all, dtype=jnp.int32)[None, :]).astype(
        jnp.int32
    )
    earlier = jnp.cumsum(one_hot, axis=0) - one_hot
    slot_rank = jnp.sum(earlier * one_hot, axis=1)
    position = targets * capacity + slot_rank
    send_values = (
        jnp.zeros((channel_count, tiles_all * capacity), jnp.float32).at[:, position].set(residual)
    )
    send_cells = jnp.zeros((tiles_all * capacity,), jnp.int32).at[position].set(trace_cell)
    got_values, got_cells = (
        lax.all_to_all(
            send_values.reshape(channel_count, tiles_all, capacity),
            ("row", "col"),
            split_axis=1,
            concat_axis=1,
            tiled=True,
        ),
        lax.all_to_all(
            send_cells.reshape(1, tiles_all, capacity),
            ("row", "col"),
            split_axis=1,
            concat_axis=1,
            tiled=True,
        ),
    )
    cotangent = (
        jnp.zeros((channel_count, RD * CD), jnp.float32)
        .at[:, got_cells.reshape(-1)]
        .add(got_values.reshape(channel_count, -1))
    )
    cotangent = cotangent.reshape(channel_count, RD, CD)
    out_slope = jax.vjp(jax.nn.gelu, pre_act)[1](cotangent)[0]
    grad_re, grad_im = local_modes(out_slope, mix_scale)
    point_part = jnp.einsum("crs,ors->co", field, out_slope, precision=exact_mode)
    bias_part = jnp.sum(out_slope, axis=(1, 2))
    modes_re, modes_im, point_sum, bias_sum = lax.psum(
        (
            widen(grad_re, C, 0),
            widen(grad_im, C, 0),
            widen(point_part, C, 1),
            widen(bias_part, C, 0),
        ),
        ("row", "col", "ch"),
    )
    own_allowed = lax.dynamic_slice_in_dim(allowed, own_first, channel_count, 0)
    own_gre = lax.dynamic_slice_in_dim(modes_re, own_first, channel_count, 0)
    own_gim = lax.dynamic_slice_in_dim(modes_im, own_first, channel_count, 0)
    grad_scale = math.sqrt(MODES / points_all)
    spec_grad_re = (
        own_allowed[None]
        * (own_gre[None] * spec_re[:, None] + own_gim[None] * spec_im[:, None])
        * grad_scale
    )
    spec_grad_im = (
        own_allowed[None]
        * (own_gim[None] * spec_re[:, None] - own_gre[None] * spec_im[:, None])
        * grad_scale
    )
    grad_spec = jnp.stack((spec_grad_re, spec_grad_im), axis=0)
    in_wre = lax.dynamic_slice_in_dim(weight_re, own_first, channel_count, 0)
    in_wim = lax.dynamic_slice_in_dim(weight_im, own_first, channel_count, 0)
    adjoint_re = jnp.sum(in_wre * modes_re[None] + in_wim * modes_im[None], axis=1)
    adjoint_im = jnp.sum(in_wre * modes_im[None] - in_wim * modes_re[None], axis=1)
    spectral_back = tile_field(adjoint_re, adjoint_im, forward_scale)
    own_point = lax.dynamic_slice_in_dim(point_weight, own_first, channel_count, 1)
    partial_back = jnp.einsum("co,ors->crs", own_point, out_slope, precision=exact_mode)
    point_back = lax.psum_scatter(partial_back, "ch", scatter_dimension=0, tiled=True)
    grad_field = point_back + spectral_back
    norm_points = 1.0 / math.sqrt(points_all)
    grad_point = lax.dynamic_slice_in_dim(point_sum, own_first, channel_count, 1) * norm_points
    grad_bias = lax.dynamic_slice_in_dim(bias_sum, own_first, channel_count, 0) * norm_points
    return (grad_field, grad_spec, grad_point, grad_bias)


def solution(mesh):
    return jax.shard_map(
        per_device,
        mesh=mesh,
        in_specs=(
            P(None, "row", "col"),
            P(),
            P(),
            P("ch"),
            P(),
            P("ch", ("row", "col")),
            P(("row", "col"), None),
            P(("row", "col")),
        ),
        out_specs=(P("ch", "row", "col"), P(None, None, "ch", None), P(None, "ch"), P("ch")),
        check_vma=False,
    )
```

profile of v0, /device:TPU:0, one launch (start us, length us, event | category | flops | bytes accessed | tf_op | source)
XLA Modules:
  0.0 457.2 jit_solution(12711133566505198467)
XLA Ops:
  7.2 0.7 fusion.42
  7.9 4.5 reduce-window.6
  12.8 0.7 fusion.41
  13.5 0.7 compare_select_fusion.1
  14.2 5.0 %scatter_custom_fusion = s32[2048]{0:T(1024)} fusion(s32[1024]{0:T(1024)S(1)} %bitcast.156, s32[1024]{0:T(1024)} %param.15, s32[]{:T(128)} %constant.114.clone.1), kind=kCustom, calls=%fused_computation.137 | custom fusion | bytes 8704 | tf_op jit(solution)/shard_map/scatter | solution.py:132
  19.3 8.3 %all-to-all-start = ((s32[1,16,128]{2,0,1:T(1,128)}), s32[1,16,128]{2,0,1:T(1,128)S(1)}, u32[]{:S(2)}, u32[]{:S(2)}) async-start(s32[1,16,128]{2,0,1:T(1,128)} %bitcast.7), calls=%async_computation | async-start | bytes 16384 | tf_op jit(solution)/shard_map/all_to_all | solution.py:141
  27.7 4.4 fusion.23
  32.1 4.4 fusion.17
  36.5 2.2 fusion.66
  38.7 2.2 fusion.68
  40.9 2.2 fusion.28
  43.3 0.2 mul.415
  43.5 2.2 fusion.27
  45.9 0.2 mul.410
  46.1 0.6 copy-done.6
  46.8 14.1 %fusion.4 = f32[16,128,512]{2,0,1:T(8,128)} fusion(f32[32,128,512]{2,1,0:T(8,128)} %param.8, f32[32,32]{1,0:T(8,128)S(1)} %copy-done, s32[]{:T(128)S(6)} %select_n.97), kind=kOutput, calls=%fused_computation.7 | convolution fusion | flops 402653184 | bytes 12587012 | tf_op jit(solution)/shard_map/co,crs->ors/dot_general | solution.py:119
  61.0 2.1 bitcast_multiply_fusion.1
  63.1 1.0 copy.80
  64.1 3.7 scatter_custom_fusion.1
  67.8 0.9 copy.81
  68.8 5.3 %copy.92 = f32[16,128,512]{1,2,0:T(8,128)} copy(f32[16,128,512]{2,0,1:T(8,128)} %fusion.4) | data formatting | bytes 8388608 | tf_op jit(solution)/shard_map/co,crs->ors/dot_general | solution.py:119
  74.1 7.0 %all-to-all-start.1 = ((f32[16,16,128]{2,0,1:T(8,128)}), f32[16,16,128]{2,0,1:T(8,128)}, u32[]{:S(2)}, u32[]{:S(2)}) async-start(f32[16,16,128]{2,0,1:T(8,128)} %copy.81), calls=%async_computation.1 | async-start | bytes 262144 | tf_op jit(solution)/shard_map/all_to_all | solution.py:134
  81.1 90.1 %all-reduce.8.cloned.1.call-done = (f32[32,512]{1,0:T(8,128)}, f32[32,512]{1,0:T(8,128)}) async-done(((f32[32,512]{1,0:T(8,128)}, f32[32,512]{1,0:T(8,128)}), (f32[32,512]{1,0:T(8,128)}, f32[32,512]{1,0:T(8,128)})) %all-reduce.8.cloned.1.call-update) | async-done | bytes 131088 | tf_op jit(solution)/shard_map/psum | solution.py:108
  171.2 1.6 add_reduce_fusion.1
  172.9 2.1 fusion.64
  175.0 1.1 fusion.51
  176.2 2.3 convolution_subtract_fusion.1
  178.5 8.7 %fusion.87 = f32[16,512,128]{2,1,0:T(8,128)} fusion(f32[16,32,512]{2,1,0:T(8,128)S(1)} %convolution_subtract_fusion.1, s32[128]{0:T(128)S(1)} %iota_add_fusion.1, s32[32]{0:T(128)S(1)} %compare_select_fusion.3), kind=kOutput, calls=%fused_computation.119 | convolution fusion | flops 402710528 | bytes 5243520 | tf_op jit(solution)/shard_map/ar,cas->crs/dot_general | solution.py:88
  187.2 2.1 convolution_add_fusion.1
  189.3 0.9 bitcast_bitcast_fusion
  190.2 0.3 copy.83
  190.5 26.2 %scatter_custom_fusion.2 = f32[16,65536]{0,1:T(8,128)} fusion(s32[2048]{0:T(1024)S(1)} %bitcast.155, f32[2048,16]{1,0:T(8,128)S(1)} %copy.83, f32[]{:T(128)} %constant.118.clone.1), kind=kCustom, calls=%fused_computation.3 | custom fusion | flops 32768 | bytes 4194308 | tf_op jit(solution)/shard_map/scatter-add | solution.py:152
  216.7 19.4 %copy.93 = f32[16,128,512]{1,2,0:T(8,128)} copy(f32[16,128,512]{0,2,1:T(8,128)} %bitcast.147) | data formatting | bytes 8388608 | tf_op jit(solution)/shard_map/reshape | solution.py:154
  236.1 14.2 %fusion.227 = (f32[16]{0:T(128)S(1)}, f32[16,128,512]{1,2,0:T(8,128)}) fusion(f32[16,128,512]{1,2,0:T(8,128)} %copy.93, f32[16]{0:T(128)S(1)} %copy-done.14, f32[16,128,512]{1,2,0:T(8,128)} %copy.92, f32[16,512,128]{2,1,0:T(8,128)} %fusion.87, f32[16,32,512]{2,1,0:T(8,128)S(1)} %copy-done.3, s32[128]{0:T(128)S(1)} %iota_add_fusion.1, ...), kind=kOutput, calls=%fused_computation.252 | convolution fusion | flops 427876352 | bytes 17826560 | tf_op jit(solution)/shard_map/ar,cas->crs/dot_general | solution.py:88
  250.4 5.5 %copy.95 = f32[16,128,512]{2,0,1:T(8,128)} copy(f32[16,128,512]{1,2,0:T(8,128)} %get-tuple-element.35) | data formatting | bytes 8388608 | tf_op jit(solution)/shard_map/transpose(jvp())/add_any | solution.py:155
  255.9 6.8 %fusion.26 = f32[16,32,512]{2,1,0:T(8,128)S(1)} fusion(f32[16,128,512]{1,2,0:T(8,128)} %get-tuple-element.35, s32[128]{0:T(128)S(1)} %iota_add_fusion.1, s32[32]{0:T(128)S(1)} %compare_select_fusion.3), kind=kOutput, calls=%fused_computation.31 | convolution fusion | flops 402972672 | bytes 5243520 | tf_op jit(solution)/shard_map/ar,crs->cas/dot_general | solution.py:59
  262.7 4.6 convolution_bitcast_fusion
  267.3 2.2 fusion.59
  269.5 2.9 fusion.61
  272.4 2.9 fusion.30
  275.3 1.0 copy.99
  276.5 3.1 fusion.29
  279.7 0.2 mul.438
  280.0 0.6 copy-done.8
  280.7 11.0 %fusion.77 = f32[32,128,512]{2,0,1:T(8,128)} fusion(f32[16,128,512]{2,0,1:T(8,128)} %copy.95, f32[32,32]{1,0:T(8,128)S(1)} %copy-done, s32[]{:T(128)S(6)} %select_n.97), kind=kOutput, calls=%fused_computation.109 | convolution fusion | flops 402653184 | bytes 12587012 | tf_op jit(solution)/shard_map/co,ors->crs/dot_general | solution.py:189
  291.8 0.2 dynamic_update_slice.23
  292.0 14.4 %fusion.34 = f32[32,32]{0,1:T(8,128)S(1)} fusion(f32[32,32]{0,1:T(8,128)S(1)} %broadcast_in_dim.10, s32[]{:T(128)S(6)} %select_n.97, f32[16,128,512]{2,0,1:T(8,128)} %copy.95, f32[32,128,512]{2,1,0:T(8,128)} %param.8), kind=kOutput, calls=%fused_computation.46 | convolution fusion | flops 402653184 | bytes 12591108 | tf_op jit(solution)/shard_map/crs,ors->co/dot_general | solution.py:157
  306.4 40.2 %all-reduce = (f32[32,32]{0,1:T(8,128)S(1)}, f32[32]{0:T(128)S(1)}) all-reduce(f32[32,32]{0,1:T(8,128)S(1)} %fusion.34, f32[32]{0:T(128)S(1)} %dynamic_update_slice.23), channel_id=1, replica_groups=mesh['row'=4,'col'=4,'ch'=2] {'row','col','ch'}, use_global_device_ids=true, to_apply=%region_15.16 | all-reduce | flops 1056 | bytes 8448 | tf_op jit(solution)/shard_map/psum | solution.py:159
  346.6 0.6 dynamic-slice_multiply_fusion.1
  347.2 0.6 dynamic-slice_multiply_fusion
  347.8 55.3 %all-reduce.6.cloned.1.call-done = (f32[32,512]{1,0:T(8,128)}, f32[32,512]{1,0:T(8,128)}) async-done(((f32[32,512]{1,0:T(8,128)}, f32[32,512]{1,0:T(8,128)}), (f32[32,512]{1,0:T(8,128)}, f32[32,512]{1,0:T(8,128)})) %all-reduce.6.cloned.1.call-update) | async-done | bytes 131088 | tf_op jit(solution)/shard_map/psum | solution.py:159
  403.1 1.7 subtract_reduce_fusion
  405.0 1.1 fusion.57
  406.1 1.1 convolution_subtract_fusion
  407.2 8.3 %fusion.84 = f32[16,512,128]{2,1,0:T(8,128)} fusion(f32[16,32,512]{2,1,0:T(8,128)S(1)} %convolution_subtract_fusion, s32[128]{0:T(128)S(1)} %iota_add_fusion.1, s32[32]{0:T(128)S(1)} %compare_select_fusion.3), kind=kOutput, calls=%fused_computation.116 | convolution fusion | flops 402710528 | bytes 5243520 | tf_op jit(solution)/shard_map/ar,cas->crs/dot_general | solution.py:88
  415.5 6.0 %copy.104 = f32[16,512,128]{1,0,2:T(8,128)} copy(f32[16,512,128]{2,1,0:T(8,128)} %fusion.84) | data formatting | bytes 8388608 | tf_op jit(solution)/shard_map/ar,cas->crs/dot_general | solution.py:88
  421.5 1.1 fusion.46
  422.6 1.1 convolution_add_fusion
  423.7 8.5 %fusion.79 = f32[16,512,128]{2,1,0:T(8,128)} fusion(f32[16,32,512]{2,1,0:T(8,128)S(1)} %convolution_add_fusion, s32[128]{0:T(128)S(1)} %iota_add_fusion.1, s32[32]{0:T(128)S(1)} %compare_select_fusion.3), kind=kOutput, calls=%fused_computation.111 | convolution fusion | flops 402710528 | bytes 5243520 | tf_op jit(solution)/shard_map/ar,cas->crs/dot_general | solution.py:88
  432.2 5.5 %copy.105 = f32[16,512,128]{1,0,2:T(8,128)} copy(f32[16,512,128]{2,1,0:T(8,128)} %fusion.79) | data formatting | bytes 8388608 | tf_op jit(solution)/shard_map/ar,cas->crs/dot_general | solution.py:88
  437.8 0.3 multiply_multiply_fusion.3
  438.2 1.6 pad_maximum_fusion
  439.8 6.2 %bitcast_add_fusion = f32[16,128,512]{2,0,1:T(8,128)S(1)} fusion(f32[16,128,512]{2,0,1:T(8,128)} %reduce-scatter.2.cloned.1.call-done, f32[16,512,128]{1,0,2:T(8,128)} %copy.104, f32[16,512,128]{1,0,2:T(8,128)} %copy.105), kind=kLoop, calls=%fused_computation.17 | loop fusion | flops 3145728 | bytes 16777216 | tf_op jit(solution)/shard_map/add | solution.py:191
  446.0 4.4 copy.108
  (70 shorter events, 2.0 us)
Async XLA Ops:
  7.2 39.6 %copy-start = (f32[32,32]{1,0:T(8,128)S(1)}, f32[32,32]{1,0:T(8,128)}, u32[]{:S(2)}) copy-start(f32[32,32]{1,0:T(8,128)} %param.10) | copy-start | bytes 12292
  19.3 54.8 %all-to-all-start = ((s32[1,16,128]{2,0,1:T(1,128)}), s32[1,16,128]{2,0,1:T(1,128)S(1)}, u32[]{:S(2)}, u32[]{:S(2)}) async-start(s32[1,16,128]{2,0,1:T(1,128)} %bitcast.7), calls=%async_computation | async-start | bytes 16384 | tf_op jit(solution)/shard_map/all_to_all | solution.py:141
  27.6 143.7 %all-reduce.8.cloned.1.call-start = ((), (), s32[]{:S(2)}) async-start(), calls=%async_computation.5 | async-start | bytes 262144 | tf_op jit(solution)/shard_map/psum | solution.py:108
  46.1 0.6 copy-start.6
  46.1 0.6 copy-start.7
  46.8 14.2 %copy-start.13 = (s32[32]{0:T(128)S(1)}, s32[32]{0:T(128)}, u32[]{:S(2)}) copy-start(s32[32]{0:T(128)} %param.12) | copy-start | bytes 388
  46.8 14.2 %copy-start.2 = (f32[2,32,32,512]{3,2,1,0:T(8,128)S(1)}, f32[2,32,32,512]{3,2,1,0:T(8,128)}, u32[]{:S(2)}) copy-start(f32[2,32,32,512]{3,2,1,0:T(8,128)} %param.9) | copy-start | bytes 12582916
  61.0 2.1 copy-start.12
  74.1 115.2 %all-to-all-start.1 = ((f32[16,16,128]{2,0,1:T(8,128)}), f32[16,16,128]{2,0,1:T(8,128)}, u32[]{:S(2)}, u32[]{:S(2)}) async-start(f32[16,16,128]{2,0,1:T(8,128)} %copy.81), calls=%async_computation.1 | async-start | bytes 262144 | tf_op jit(solution)/shard_map/all_to_all | solution.py:134
  81.1 322.0 %all-reduce.6.cloned.1.call-start = ((), (), s32[]{:S(2)}) async-start(), calls=%async_computation.4 | async-start | bytes 262144 | tf_op jit(solution)/shard_map/psum | solution.py:159
  216.7 19.5 %copy-start.3 = (f32[16,32,512]{2,1,0:T(8,128)S(1)}, f32[16,32,512]{2,1,0:T(8,128)}, u32[]{:S(2)}) copy-start(f32[16,32,512]{2,1,0:T(8,128)} %convolution_add_fusion.1) | copy-start | bytes 3145732
  216.7 19.5 %copy-start.14 = (f32[16]{0:T(128)S(1)}, f32[16]{0:T(128)}, u32[]{:S(2)}) copy-start(f32[16]{0:T(128)} %param.11) | copy-start | bytes 196
  255.9 6.8 %copy-start.1 = (f32[16,128,512]{1,2,0:T(8,128)S(1)}, f32[16,128,512]{1,2,0:T(8,128)}, u32[]{:S(2)}) copy-start(f32[16,128,512]{1,2,0:T(8,128)} %get-tuple-element.35) | copy-start | bytes 12582916
  279.9 0.6 copy-start.8
  280.0 0.6 copy-start.9
  280.6 159.2 %reduce-scatter.2.cloned.1.call-start = ((), (), s32[]{:S(2)}) async-start(), calls=%async_computation.3 | async-start | bytes 12582912 | tf_op jit(solution)/shard_map/reduce_scatter | solution.py:190
  432.2 5.6 %copy-start.11 = (f32[32,512]{1,0:T(8,128)S(1)}, f32[32,512]{1,0:T(8,128)}, u32[]{:S(2)}) copy-start(f32[32,512]{1,0:T(8,128)} %get-tuple-element.26) | copy-start | bytes 196612
  432.2 5.6 %copy-start.10 = (f32[32,512]{1,0:T(8,128)S(1)}, f32[32,512]{1,0:T(8,128)}, u32[]{:S(2)}) copy-start(f32[32,512]{1,0:T(8,128)} %get-tuple-element.27) | copy-start | bytes 196612
  432.2 5.6 %copy-start.4 = (f32[32,512]{1,0:T(8,128)S(1)}, f32[32,512]{1,0:T(8,128)}, u32[]{:S(2)}) copy-start(f32[32,512]{1,0:T(8,128)} %get-tuple-element.28) | copy-start | bytes 196612
  432.2 5.6 %copy-start.5 = (f32[32,512]{1,0:T(8,128)S(1)}, f32[32,512]{1,0:T(8,128)}, u32[]{:S(2)}) copy-start(f32[32,512]{1,0:T(8,128)} %get-tuple-element.29) | copy-start | bytes 196612
Sparse Core Ops, SparseCore 0:
  46.9 124.3 all-reduce.7
  280.7 122.2 all-reduce.5
  405.4 15.7 reduce-scatter.1
where the time goes:
time: 465 us; the launch traced here: 457 us
  waiting for transfers between devices  145 us (31%)
  matrix products  131 us (28%)
  local copies, waits for them, and re-layouts  62.7 us (13%)
  other arithmetic  47.6 us (10%)
  blocking collectives  40.2 us (9%)
  starting transfers between devices  15.4 us (3%)
  between operations  14.5 us (3%)
    psum x1, waiting for transfers between devices, per_device(): lax.psum((widen(part_re, C, 0), widen(part_im, C, 0)), ('row', 'col', 'ch'))  90.1 us
    psum x1, waiting for transfers between devices, per_device(): lax.psum((widen(grad_re, C, 0), widen(grad_im, C, 0), widen(point_part, C...  55.3 us
    psum x1, blocking collectives, per_device(): lax.psum((widen(grad_re, C, 0), widen(grad_im, C, 0), widen(point_part, C...  40.2 us
    scatter-add x1, other arithmetic, per_device(): cotangent = jnp.zeros((channel_count, RD * CD), jnp.float32).at[:, got_ce...  26.2 us
    dot_general x2, matrix products, tile_field(): jnp.einsum('ar,cas->crs', sin_rows, half_im, precision=exact_mode)  22.7 us
    reshape x1, local copies, waits for them, and re-layouts, per_device(): cotangent = cotangent.reshape(channel_count, RD, CD)  19.4 us
    dot_general x2, matrix products, tile_field(): jnp.einsum('ar,cas->crs', cos_rows, half_re, precision=exact_mode)  17 us
    dot_general x1, matrix products, per_device(): jnp.einsum('crs,ors->co', field, out_slope, precision=exact_mode)  14.4 us
  transfers between devices with their start and end apart: 5, of which 2 were waited for; matrix products, arithmetic and copies ran while one was open for 28% of the time, Pallas kernels for 0%

commit v1 on v0

--- a/solution.py
+++ b/solution.py
@@ -3,6 +3,7 @@
 import jax.numpy as jnp
 from jax import lax
 from jax.sharding import PartitionSpec as P
+from jax.lax import psum
 
 C = 32
 M = 16
@@ -156,14 +157,17 @@
     grad_re, grad_im = local_modes(out_slope, mix_scale)
     point_part = jnp.einsum("crs,ors->co", field, out_slope, precision=exact_mode)
     bias_part = jnp.sum(out_slope, axis=(1, 2))
-    modes_re, modes_im, point_sum, bias_sum = lax.psum(
-        (
-            widen(grad_re, C, 0),
-            widen(grad_im, C, 0),
-            widen(point_part, C, 1),
-            widen(bias_part, C, 0),
-        ),
-        ("row", "col", "ch"),
+    modes_re, modes_im, point_sum, bias_sum = psum(
+        psum(
+            (
+                widen(grad_re, C, 0),
+                widen(grad_im, C, 0),
+                widen(point_part, C, 1),
+                widen(bias_part, C, 0),
+            ),
+            ("col", "ch"),
+        ),
+        "row",
     )
     own_allowed = lax.dynamic_slice_in_dim(allowed, own_first, channel_count, 0)
     own_gre = lax.dynamic_slice_in_dim(modes_re, own_first, channel_count, 0)

time: 465 us -> 454 us (0.976)
  waiting for transfers between devices: 145 us -> 137 us
    psum x1 -> x2, waiting for transfers between devices: 55.3 us -> 46.6 us  [the longest x1 46.6 us: per_device(): psum((widen(grad_re, C, 0), widen(grad_im, C, 0), widen(point_part, C, 1)...]
    psum x1 -> x2, blocking collectives: 40.2 us -> 41.9 us  [the longest x1 22.3 us: per_device(): psum((widen(grad_re, C, 0), widen(grad_im, C, 0), widen(point_part, C, 1)...]
  transfers between devices with their start and end apart: 5 -> 6, of which waited for: 2 -> 2; matrix products, arithmetic and copies ran while one was open for 28% -> 30% of each run, Pallas kernels for 0% -> 0%
where the time goes in v1:
time: 454 us; the launch traced here: 446 us
  waiting for transfers between devices  137 us (30%)
  matrix products  127 us (28%)
  local copies, waits for them, and re-layouts  62.7 us (14%)
  other arithmetic  47.6 us (10%)
  blocking collectives  41.9 us (9%)
  starting transfers between devices  15.4 us (3%)
  between operations  14.5 us (3%)
    psum x1, waiting for transfers between devices, per_device(): lax.psum((widen(part_re, C, 0), widen(part_im, C, 0)), ('row', 'col', 'ch'))  90.1 us
    psum x1, waiting for transfers between devices, per_device(): psum((widen(grad_re, C, 0), widen(grad_im, C, 0), widen(point_part, C, 1)...  46.6 us
    scatter-add x1, other arithmetic, per_device(): cotangent = jnp.zeros((channel_count, RD * CD), jnp.float32).at[:, got_ce...  26.2 us
    psum x1, blocking collectives, per_device(): psum((widen(grad_re, C, 0), widen(grad_im, C, 0), widen(point_part, C, 1)...  22.3 us
    dot_general x2, matrix products, tile_field(): jnp.einsum('ar,cas->crs', sin_rows, half_im, precision=exact_mode)  21.5 us
    psum x1, blocking collectives, per_device(): psum(psum((widen(grad_re, C, 0), widen(grad_im, C, 0), widen(point_part,...  19.5 us
    reshape x1, local copies, waits for them, and re-layouts, per_device(): cotangent = cotangent.reshape(channel_count, RD, CD)  19.4 us
    dot_general x2, matrix products, tile_field(): jnp.einsum('ar,cas->crs', cos_rows, half_re, precision=exact_mode)  17 us
  transfers between devices with their start and end apart: 6, of which 2 were waited for; matrix products, arithmetic and copies ran while one was open for 30% of the time, Pallas kernels for 0%

profile of v1, /device:TPU:0, one launch (start us, length us, event | category | flops | bytes accessed | tf_op | source)
XLA Modules:
  0.0 446.3 jit_solution(15664604771785301083)
XLA Ops:
  7.2 0.7 fusion.42
  7.9 4.5 %reduce-window.6 = s32[16,8,128]{2,1,0:T(8,128)S(1)} reduce-window(s32[16,8,128]{2,1,0:T(8,128)S(1)} %fusion.42, s32[]{:T(128)} %constant.114.clone.1), window={size=1x1x128 pad=0_0x0_0x127_0}, to_apply=%region_0.1 | reduce-window | flops 2080768 | bytes 131076 | tf_op jit(solution)/shard_map/reduce-window
  12.8 0.7 fusion.41
  13.5 0.7 compare_select_fusion.1
  14.2 5.0 %scatter_custom_fusion = s32[2048]{0:T(1024)} fusion(s32[1024]{0:T(1024)S(1)} %bitcast.156, s32[1024]{0:T(1024)} %param.15, s32[]{:T(128)} %constant.114.clone.1), kind=kCustom, calls=%fused_computation.137 | custom fusion | bytes 8704 | tf_op jit(solution)/shard_map/scatter | solution.py:133
  19.3 8.3 %all-to-all-start = ((s32[1,16,128]{2,0,1:T(1,128)}), s32[1,16,128]{2,0,1:T(1,128)S(1)}, u32[]{:S(2)}, u32[]{:S(2)}) async-start(s32[1,16,128]{2,0,1:T(1,128)} %bitcast.7), calls=%async_computation | async-start | bytes 16384 | tf_op jit(solution)/shard_map/all_to_all | solution.py:142
  27.7 4.4 fusion.23
  32.1 4.4 fusion.17
  36.5 2.2 fusion.66
  38.7 2.2 fusion.68
  40.9 2.2 fusion.28
  43.3 0.2 mul.415
  43.5 2.2 fusion.27
  46.1 0.6 copy-done.6
  46.8 14.1 %fusion.4 = f32[16,128,512]{2,0,1:T(8,128)} fusion(f32[32,128,512]{2,1,0:T(8,128)} %param.8, f32[32,32]{1,0:T(8,128)S(1)} %copy-done, s32[]{:T(128)S(6)} %select_n.97), kind=kOutput, calls=%fused_computation.7 | convolution fusion | flops 402653184 | bytes 12587012 | tf_op jit(solution)/shard_map/co,crs->ors/dot_general | solution.py:120
  61.0 2.1 bitcast_multiply_fusion.1
  63.1 1.0 copy.80
  64.1 3.7 scatter_custom_fusion.1
  67.8 0.9 copy.81
  68.8 5.3 %copy.92 = f32[16,128,512]{1,2,0:T(8,128)} copy(f32[16,128,512]{2,0,1:T(8,128)} %fusion.4) | data formatting | bytes 8388608 | tf_op jit(solution)/shard_map/co,crs->ors/dot_general | solution.py:120
  74.1 7.0 %all-to-all-start.1 = ((f32[16,16,128]{2,0,1:T(8,128)}), f32[16,16,128]{2,0,1:T(8,128)}, u32[]{:S(2)}, u32[]{:S(2)}) async-start(f32[16,16,128]{2,0,1:T(8,128)} %copy.81), calls=%async_computation.1 | async-start | bytes 262144 | tf_op jit(solution)/shard_map/all_to_all | solution.py:135
  81.1 90.1 %all-reduce.9.cloned.1.call-done = (f32[32,512]{1,0:T(8,128)}, f32[32,512]{1,0:T(8,128)}) async-done(((f32[32,512]{1,0:T(8,128)}, f32[32,512]{1,0:T(8,128)}), (f32[32,512]{1,0:T(8,128)}, f32[32,512]{1,0:T(8,128)})) %all-reduce.9.cloned.1.call-update) | async-done | bytes 131088 | tf_op jit(solution)/shard_map/psum | solution.py:109
  171.2 1.6 add_reduce_fusion.1
  172.9 2.1 fusion.64
  175.0 1.1 fusion.51
  176.2 2.3 convolution_subtract_fusion.1
  178.5 8.7 %fusion.87 = f32[16,512,128]{2,1,0:T(8,128)} fusion(f32[16,32,512]{2,1,0:T(8,128)S(1)} %convolution_subtract_fusion.1, s32[128]{0:T(128)S(1)} %iota_add_fusion.1, s32[32]{0:T(128)S(1)} %compare_select_fusion.3), kind=kOutput, calls=%fused_computation.119 | convolution fusion | flops 402710528 | bytes 5243520 | tf_op jit(solution)/shard_map/ar,cas->crs/dot_general | solution.py:89
  187.2 2.1 convolution_add_fusion.1
  189.3 0.9 bitcast_bitcast_fusion
  190.2 0.3 copy.83
  190.5 26.2 %scatter_custom_fusion.2 = f32[16,65536]{0,1:T(8,128)} fusion(s32[2048]{0:T(1024)S(1)} %bitcast.155, f32[2048,16]{1,0:T(8,128)S(1)} %copy.83, f32[]{:T(128)} %constant.118.clone.1), kind=kCustom, calls=%fused_computation.3 | custom fusion | flops 32768 | bytes 4194308 | tf_op jit(solution)/shard_map/scatter-add | solution.py:153
  216.7 19.4 %copy.93 = f32[16,128,512]{1,2,0:T(8,128)} copy(f32[16,128,512]{0,2,1:T(8,128)} %bitcast.147) | data formatting | bytes 8388608 | tf_op jit(solution)/shard_map/reshape | solution.py:155
  236.1 13.0 %fusion.227 = (f32[16]{0:T(128)S(1)}, f32[16,128,512]{1,2,0:T(8,128)S(1)}) fusion(f32[16,128,512]{1,2,0:T(8,128)} %copy.93, f32[16]{0:T(128)S(1)} %copy-done.14, f32[16,128,512]{1,2,0:T(8,128)} %copy.92, f32[16,512,128]{2,1,0:T(8,128)} %fusion.87, f32[16,32,512]{2,1,0:T(8,128)S(1)} %copy-done.3, s32[128]{0:T(128)S(1)} %iota_add_fusion.1, ...), kind=kOutput, calls=%fused_computation.252 | convolution fusion | flops 427876352 | bytes 17826560 | tf_op jit(solution)/shard_map/ar,cas->crs/dot_general | solution.py:89
  249.1 4.6 %fusion.26 = f32[16,32,512]{2,1,0:T(8,128)S(1)} fusion(f32[16,128,512]{1,2,0:T(8,128)S(1)} %get-tuple-element.39, s32[128]{0:T(128)S(1)} %iota_add_fusion.1, s32[32]{0:T(128)S(1)} %compare_select_fusion.3), kind=kOutput, calls=%fused_computation.31 | convolution fusion | flops 402972672 | bytes 5243520 | tf_op jit(solution)/shard_map/ar,crs->cas/dot_general | solution.py:60
  253.7 4.5 %convolution_bitcast_fusion = f32[16,32,512]{2,1,0:T(8,128)S(1)} fusion(f32[16,128,512]{1,2,0:T(8,128)S(1)} %get-tuple-element.39, s32[128]{0:T(128)S(1)} %iota_add_fusion.1, s32[32]{0:T(128)S(1)} %compare_select_fusion.3), kind=kOutput, calls=%fused_computation.32 | convolution fusion | flops 402710528 | bytes 5243520 | tf_op jit(solution)/shard_map/ar,crs->cas/dot_general | solution.py:59
  258.3 2.2 fusion.59
  260.5 2.9 fusion.61
  263.4 2.9 fusion.30
  266.3 1.0 copy.99
  267.5 3.1 fusion.29
  270.6 0.2 copy.98
  271.0 0.6 copy-done.8
  271.6 5.9 %copy.95 = f32[16,128,512]{2,0,1:T(8,128)} copy(f32[16,128,512]{1,2,0:T(8,128)} %copy-done.1) | data formatting | bytes 8388608 | tf_op jit(solution)/shard_map/transpose(jvp())/add_any | solution.py:156
  277.6 46.6 %all-reduce.11.cloned.1.call-done = (f32[32,512]{1,0:T(8,128)}, f32[32,512]{1,0:T(8,128)}) async-done(((f32[32,512]{1,0:T(8,128)}, f32[32,512]{1,0:T(8,128)}), (f32[32,512]{1,0:T(8,128)}, f32[32,512]{1,0:T(8,128)})) %all-reduce.11.cloned.1.call-update) | async-done | bytes 131088 | tf_op jit(solution)/shard_map/psum | solution.py:161
  324.3 10.6 %fusion.77 = f32[32,128,512]{2,0,1:T(8,128)} fusion(f32[16,128,512]{2,0,1:T(8,128)} %copy.95, f32[32,32]{1,0:T(8,128)S(1)} %copy-done, s32[]{:T(128)S(6)} %select_n.97), kind=kOutput, calls=%fused_computation.109 | convolution fusion | flops 402653184 | bytes 12587012 | tf_op jit(solution)/shard_map/co,ors->crs/dot_general | solution.py:193
  335.0 0.2 dynamic_update_slice.23
  335.2 14.4 %fusion.34 = f32[32,32]{0,1:T(8,128)S(1)} fusion(f32[32,32]{0,1:T(8,128)S(1)} %broadcast_in_dim.10, s32[]{:T(128)S(6)} %select_n.97, f32[16,128,512]{2,0,1:T(8,128)} %copy.95, f32[32,128,512]{2,1,0:T(8,128)} %param.8), kind=kOutput, calls=%fused_computation.46 | convolution fusion | flops 402653184 | bytes 12591108 | tf_op jit(solution)/shard_map/crs,ors->co/dot_general | solution.py:158
  349.7 22.3 %all-reduce.1 = (f32[32,32]{0,1:T(8,128)S(1)}, f32[32]{0:T(128)S(1)}) all-reduce(f32[32,32]{0,1:T(8,128)S(1)} %fusion.34, f32[32]{0:T(128)S(1)} %dynamic_update_slice.23), channel_id=1, replica_groups=mesh['row'=4,'col'=4,'ch'=2] {'col','ch'}, use_global_device_ids=true, to_apply=%region_17.18 | all-reduce | flops 1056 | bytes 8448 | tf_op jit(solution)/shard_map/psum | solution.py:161
  372.0 19.5 %all-reduce.3 = (f32[32,32]{0,1:T(8,128)S(1)}, f32[32]{0:T(128)S(1)}) all-reduce(f32[32,32]{0,1:T(8,128)S(1)} %get-tuple-element.26, f32[32]{0:T(128)S(1)} %get-tuple-element.27), channel_id=1, replica_groups=mesh['row'=4,'col'=4,'ch'=2] {'row'}, use_global_device_ids=true, to_apply=%region_18.19 | all-reduce | flops 1056 | bytes 8448 | tf_op jit(solution)/shard_map/psum | solution.py:160
  391.5 0.6 dynamic-slice_multiply_fusion.1
  392.1 0.6 dynamic-slice_multiply_fusion
  392.7 1.7 subtract_reduce_fusion
  394.6 1.1 fusion.57
  395.7 1.1 convolution_subtract_fusion
  396.8 8.3 %fusion.84 = f32[16,512,128]{2,1,0:T(8,128)} fusion(f32[16,32,512]{2,1,0:T(8,128)S(1)} %convolution_subtract_fusion, s32[128]{0:T(128)S(1)} %iota_add_fusion.1, s32[32]{0:T(128)S(1)} %compare_select_fusion.3), kind=kOutput, calls=%fused_computation.116 | convolution fusion | flops 402710528 | bytes 5243520 | tf_op jit(solution)/shard_map/ar,cas->crs/dot_general | solution.py:89
  405.1 5.5 %copy.104 = f32[16,512,128]{1,0,2:T(8,128)} copy(f32[16,512,128]{2,1,0:T(8,128)} %fusion.84) | data formatting | bytes 8388608 | tf_op jit(solution)/shard_map/ar,cas->crs/dot_general | solution.py:89
  410.6 1.1 fusion.46
  411.7 1.1 convolution_add_fusion
  412.9 8.5 %fusion.79 = f32[16,512,128]{2,1,0:T(8,128)} fusion(f32[16,32,512]{2,1,0:T(8,128)S(1)} %convolution_add_fusion, s32[128]{0:T(128)S(1)} %iota_add_fusion.1, s32[32]{0:T(128)S(1)} %compare_select_fusion.3), kind=kOutput, calls=%fused_computation.111 | convolution fusion | flops 402710528 | bytes 5243520 | tf_op jit(solution)/shard_map/ar,cas->crs/dot_general | solution.py:89
  421.4 5.5 %copy.105 = f32[16,512,128]{1,0,2:T(8,128)} copy(f32[16,512,128]{2,1,0:T(8,128)} %fusion.79) | data formatting | bytes 8388608 | tf_op jit(solution)/shard_map/ar,cas->crs/dot_general | solution.py:89
  427.0 0.3 multiply_multiply_fusion.3
  427.3 1.6 pad_maximum_fusion
  428.9 6.2 %bitcast_add_fusion = f32[16,128,512]{2,0,1:T(8,128)S(1)} fusion(f32[16,128,512]{2,0,1:T(8,128)} %reduce-scatter.2.cloned.1.call-done, f32[16,512,128]{1,0,2:T(8,128)} %copy.104, f32[16,512,128]{1,0,2:T(8,128)} %copy.105), kind=kLoop, calls=%fused_computation.17 | loop fusion | flops 3145728 | bytes 16777216 | tf_op jit(solution)/shard_map/add | solution.py:195
  435.1 4.4 copy.108
  (74 shorter events, 2.2 us)
Async XLA Ops:
  7.2 39.6 %copy-start = (f32[32,32]{1,0:T(8,128)S(1)}, f32[32,32]{1,0:T(8,128)}, u32[]{:S(2)}) copy-start(f32[32,32]{1,0:T(8,128)} %param.10) | copy-start | bytes 12292
  19.3 54.8 %all-to-all-start = ((s32[1,16,128]{2,0,1:T(1,128)}), s32[1,16,128]{2,0,1:T(1,128)S(1)}, u32[]{:S(2)}, u32[]{:S(2)}) async-start(s32[1,16,128]{2,0,1:T(1,128)} %bitcast.7), calls=%async_computation | async-start | bytes 16384 | tf_op jit(solution)/shard_map/all_to_all | solution.py:142
  27.6 143.7 %all-reduce.9.cloned.1.call-start = ((), (), s32[]{:S(2)}) async-start(), calls=%async_computation.4 | async-start | bytes 262144 | tf_op jit(solution)/shard_map/psum | solution.py:109
  46.1 0.6 copy-start.6
  46.1 0.6 copy-start.7
  46.8 14.2 %copy-start.13 = (s32[32]{0:T(128)S(1)}, s32[32]{0:T(128)}, u32[]{:S(2)}) copy-start(s32[32]{0:T(128)} %param.12) | copy-start | bytes 388
  46.8 14.2 %copy-start.2 = (f32[2,32,32,512]{3,2,1,0:T(8,128)S(1)}, f32[2,32,32,512]{3,2,1,0:T(8,128)}, u32[]{:S(2)}) copy-start(f32[2,32,32,512]{3,2,1,0:T(8,128)} %param.9) | copy-start | bytes 12582916
  61.0 2.1 copy-start.12
  74.1 115.2 %all-to-all-start.1 = ((f32[16,16,128]{2,0,1:T(8,128)}), f32[16,16,128]{2,0,1:T(8,128)}, u32[]{:S(2)}, u32[]{:S(2)}) async-start(f32[16,16,128]{2,0,1:T(8,128)} %copy.81), calls=%async_computation.1 | async-start | bytes 262144 | tf_op jit(solution)/shard_map/all_to_all | solution.py:135
  81.1 243.2 %all-reduce.11.cloned.1.call-start = ((), (), s32[]{:S(2)}) async-start(), calls=%async_computation.5 | async-start | bytes 262144 | tf_op jit(solution)/shard_map/psum | solution.py:161
  216.7 19.5 %copy-start.3 = (f32[16,32,512]{2,1,0:T(8,128)S(1)}, f32[16,32,512]{2,1,0:T(8,128)}, u32[]{:S(2)}) copy-start(f32[16,32,512]{2,1,0:T(8,128)} %convolution_add_fusion.1) | copy-start | bytes 3145732
  216.7 19.5 %copy-start.14 = (f32[16]{0:T(128)S(1)}, f32[16]{0:T(128)}, u32[]{:S(2)}) copy-start(f32[16]{0:T(128)} %param.11) | copy-start | bytes 196
  249.1 9.1 %copy-start.1 = (f32[16,128,512]{1,2,0:T(8,128)}, f32[16,128,512]{1,2,0:T(8,128)S(1)}, u32[]{:S(2)}) copy-start(f32[16,128,512]{1,2,0:T(8,128)S(1)} %get-tuple-element.39) | copy-start | bytes 12582916
  270.9 0.6 copy-start.8
  271.0 0.6 copy-start.9
  271.6 121.1 %all-reduce.13.cloned.1.call-start = ((), (), s32[]{:S(2)}) async-start(), calls=%async_computation.6 | async-start | bytes 262144 | tf_op jit(solution)/shard_map/psum | solution.py:160
  324.2 104.6 %reduce-scatter.2.cloned.1.call-start = ((), (), s32[]{:S(2)}) async-start(), calls=%async_computation.3 | async-start | bytes 12582912 | tf_op jit(solution)/shard_map/reduce_scatter | solution.py:194
  421.4 5.6 %copy-start.11 = (f32[32,512]{1,0:T(8,128)S(1)}, f32[32,512]{1,0:T(8,128)}, u32[]{:S(2)}) copy-start(f32[32,512]{1,0:T(8,128)} %get-tuple-element.32) | copy-start | bytes 196612
  421.4 5.6 %copy-start.10 = (f32[32,512]{1,0:T(8,128)S(1)}, f32[32,512]{1,0:T(8,128)}, u32[]{:S(2)}) copy-start(f32[32,512]{1,0:T(8,128)} %get-tuple-element.33) | copy-start | bytes 196612
  421.4 5.6 %copy-start.4 = (f32[32,512]{1,0:T(8,128)S(1)}, f32[32,512]{1,0:T(8,128)}, u32[]{:S(2)}) copy-start(f32[32,512]{1,0:T(8,128)} %get-tuple-element.24) | copy-start | bytes 196612
  421.4 5.6 %copy-start.5 = (f32[32,512]{1,0:T(8,128)S(1)}, f32[32,512]{1,0:T(8,128)}, u32[]{:S(2)}) copy-start(f32[32,512]{1,0:T(8,128)} %get-tuple-element.25) | copy-start | bytes 196612
Sparse Core Ops, SparseCore 0:
  46.9 124.3 all-reduce.8
  271.7 52.4 all-reduce.10
  326.7 33.9 all-reduce.12
  362.8 16.4 reduce-scatter.1
